TPU v7x, 512 devices: a whole 4x8x8 slice. The times are simulated.
512 devices in a mesh: tile: 128 (over y, z, core), clip: 4 (over x).
Axes of the slice: x: 4, y: 8, z: 8, core: 2. Of those that a mesh axis runs over, the one named last changes fastest.
Arguments:
- features: bfloat16 [4, 128, 96, 3, 4096], P('clip', 'tile'), may hold values from -6 to 6
- conv_weight: bfloat16 [3, 9, 3, 96], replicated, may hold values from -0.125 to 0.125
- bias: float32 [3], replicated, may hold values from -2 to 2
- blend_profile: int32 [32], replicated, may hold values from 1 to 8
- tile_ids: int32 [4, 128], P('clip'), may hold values from 0 to 127, each once within a row
- reward_grad: bfloat16 [4, 128, 3, 4096], P('clip', 'tile'), may hold values from -6 to 6
Outputs:
- decoded: bfloat16 [4, 128, 3, 4096], P('clip', 'tile')
- feature_grad: bfloat16 [4, 128, 96, 3, 4096], P('clip', 'tile')
- weight_grad: float32 [3, 9, 3, 96], replicated
- bias_grad: float32 [3], replicated
Inputs may be any that keep to these rules, and one draw needn't show every extreme that they name: Each row of tile_ids names each of the 128 tiles of the window once; tile v lies in tile row v // 16 and tile column v % 16.
All inputs are finite; a program needn't handle non-finite values.
Results may differ from a plain program's by a relative error of at most 0.023.
Values may be sent and summed in bfloat16 or wider, within the bound.
No kernel may reach another device: no remote copies, remote signals or barrier semaphores. Data moves between devices by JAX's collectives and lax.ppermute only.
A program may use at most 64 MiB of HBM per device.

v0:
```python
import math
import jax
import jax.numpy as jnp
from jax import lax
from jax.sharding import PartitionSpec as P

neighbour_steps = [(-1, -1), (-1, 0), (-1, 1), (0, -1), (0, 1), (1, -1), (1, 0), (1, 1)]


def cut_region(tile_block, step_y, step_x, intersection):
    edge = tile_block.shape[-1]
    if step_y == 1:
        tile_block = tile_block[..., :intersection, :]
    elif step_y == -1:
        tile_block = tile_block[..., edge - intersection :, :]
    if step_x == 1:
        tile_block = tile_block[..., :intersection]
    elif step_x == -1:
        tile_block = tile_block[..., edge - intersection :]
    return tile_block


def place_region(region, step_y, step_x, stride):
    pad_y = (stride, 0) if step_y == 1 else (0, stride) if step_y == -1 else (0, 0)
    pad_x = (stride, 0) if step_x == 1 else (0, stride) if step_x == -1 else (0, 0)
    return jnp.pad(region, ((0, 0),) * (region.ndim - 2) + (pad_y, pad_x))


def pick_regions(gathered, neighbours, intersection, edge):
    regions = []
    for step_y, step_x, present, holder in neighbours:
        whole_tile = lax.dynamic_index_in_dim(gathered, holder, keepdims=False)
        whole_tile = whole_tile.reshape(whole_tile.shape[0], edge, edge)
        regions.append(cut_region(whole_tile, step_y, step_x, intersection))
    return regions


def per_device(features, conv_weight, bias, blend_profile, tile_ids, reward_grad):
    pixels = features.shape[-1]
    edge = math.isqrt(pixels)
    intersection = blend_profile.shape[0]
    stride = edge - intersection
    colours = conv_weight.shape[2]
    channels = conv_weight.shape[3]
    slots = tile_ids.shape[1]
    own_index = lax.axis_index("tile")
    peer_count = lax.axis_size("tile")
    tiles_across = min(16, peer_count)
    tile_count_rows = slots // tiles_across
    tile_list = tile_ids[0]
    mine = lax.dynamic_index_in_dim(tile_list, own_index, keepdims=False)
    my_row = mine // tiles_across
    my_col = mine % tiles_across
    places = jnp.arange(slots, dtype=jnp.int32)
    neighbours = []
    for step_y, step_x in neighbour_steps:
        tile_row = my_row + step_y
        tile_col = my_col + step_x
        present = (
            (tile_row >= 0)
            & (tile_row < tile_count_rows)
            & (tile_col >= 0)
            & (tile_col < tiles_across)
        )
        target = tile_row * tiles_across + tile_col
        holder = jnp.sum(jnp.where(tile_list == target, places, 0))
        neighbours.append((step_y, step_x, present, holder))
    distance_range = jnp.arange(edge)
    distance = jnp.minimum(jnp.minimum(distance_range, edge - 1 - distance_range), intersection - 1)
    lookup = (distance[:, None] == jnp.arange(intersection)[None, :]).astype(jnp.float32)
    factor = jnp.dot(lookup, blend_profile.astype(jnp.float32))
    weight_map = factor[:, None] * factor[None, :]
    frames = features[0, 0]
    kernel = conv_weight.reshape(conv_weight.shape[0], 9 * colours, channels)
    tap_sums = jnp.einsum("tjc,ctp->jp", kernel, frames, preferred_element_type=jnp.float32)
    tap_sums = tap_sums.reshape(3, 3, colours, edge, edge)
    padded = jnp.pad(tap_sums, ((0, 0), (0, 0), (0, 0), (1, 1), (1, 1)))
    tile_image = jnp.broadcast_to(bias[:, None, None], (colours, edge, edge))
    for shift_y in range(3):
        for shift_x in range(3):
            tile_image = (
                tile_image
                + padded[shift_y, shift_x, :, shift_y : shift_y + edge, shift_x : shift_x + edge]
            )
    tile_image = tile_image.astype(jnp.bfloat16)
    cotangent = reward_grad[0, 0]
    gathered_images = lax.all_gather(
        tile_image.reshape(1, colours, pixels), "tile", axis=0, tiled=True
    )
    gathered_grads = lax.all_gather(
        cotangent.reshape(1, colours, pixels), "tile", axis=0, tiled=True
    )
    forward_regions = pick_regions(gathered_images, neighbours, intersection, edge)
    backward_regions = pick_regions(gathered_grads, neighbours, intersection, edge)
    numerator = weight_map * tile_image.astype(jnp.float32)
    weight_total = weight_map
    summed = cotangent.astype(jnp.float32).reshape(colours, edge, edge)
    for (step_y, step_x, present, holder), image_part, grad_part in zip(
        neighbours, forward_regions, backward_regions
    ):
        present_mask = present.astype(jnp.float32)
        part_weight = place_region(
            cut_region(weight_map, step_y, step_x, intersection), step_y, step_x, stride
        )
        numerator = numerator + present_mask * part_weight * place_region(
            image_part.astype(jnp.float32), step_y, step_x, stride
        )
        weight_total = weight_total + present_mask * part_weight
        summed = summed + present_mask * place_region(
            grad_part.astype(jnp.float32), step_y, step_x, stride
        )
    decoded = (numerator / weight_total).astype(jnp.bfloat16).reshape(1, 1, colours, pixels)
    image_grad = (weight_map / weight_total * summed).astype(jnp.bfloat16)
    grad_padded = jnp.pad(image_grad, ((0, 0), (1, 1), (1, 1)))
    shifted = []
    for shift_y in range(3):
        for shift_x in range(3):
            shifted.append(
                grad_padded[:, 2 - shift_y : 2 - shift_y + edge, 2 - shift_x : 2 - shift_x + edge]
            )
    grad_stack = jnp.stack(shifted, 0).reshape(9 * colours, pixels)
    value_grad = jnp.einsum("tjc,jp->ctp", kernel, grad_stack, preferred_element_type=jnp.float32)
    feature_grad = value_grad.astype(jnp.bfloat16).reshape(1, 1, channels, frames.shape[1], pixels)
    kernel_local = jnp.einsum("jp,ctp->tjc", grad_stack, frames, preferred_element_type=jnp.float32)
    bias_local = jnp.sum(image_grad.astype(jnp.float32), axis=(1, 2))
    kernel_total, bias_total = lax.psum((kernel_local, bias_local), ("tile", "clip"))
    grad_scale = 1.0 / math.sqrt(lax.axis_size("clip") * lax.axis_size("tile") * pixels)
    weight_grad = (kernel_total * grad_scale).reshape(conv_weight.shape[0], 9, colours, channels)
    bias_grad = bias_total * grad_scale
    return (decoded, feature_grad, weight_grad, bias_grad)


def solution(mesh):
    return jax.shard_map(
        per_device,
        mesh=mesh,
        in_specs=(
            P("clip", "tile", None, None, None),
            P(),
            P(),
            P(),
            P("clip", None),
            P("clip", "tile", None, None),
        ),
        out_specs=(P("clip", "tile", None, None), P("clip", "tile", None, None, None), P(), P()),
        check_vma=False,
    )
```

profile of v0, /device:TPU:1, one launch (start us, length us, event | category | flops | bytes accessed | tf_op | source)
XLA Modules:
  0.0 295.1 jit_solution(15663109818594018392)
XLA Ops:
  7.2 0.7 all-gather.6.cloned.1.call-update
  8.0 4.5 %copy.34 = bf16[1,1,96,3,4096]{2,4,3,1,0:T(8,128)(2,1)} copy(bf16[1,1,96,3,4096]{4,2,3,1,0:T(8,128)(2,1)} %param.6) | data formatting | bytes 4718592 | tf_op args[0]
  12.6 0.6 copy-done.3
  13.1 4.0 %fusion.5 = f32[3,3,3,64,64]{4,2,3,1,0:T(4,128)S(1)} fusion(bf16[64,64,96,3,1,1]{2,1,0,3,5,4:T(8,128)(2,1)} %bitcast.182, bf16[3,3,3,96,3]{3,2,1,0,4:T(4,128)(2,1)S(1)} %dot_general.22), kind=kOutput, calls=%fused_computation.6 | convolution fusion | flops 63700992 | bytes 2817216 | tf_op jit(solution)/shard_map/tjc,ctp->jp/dot_general | solution.py:75
  17.2 0.5 pad_slice_fusion.7
  17.7 0.1 squeeze.90
  17.8 0.1 squeeze.89
  18.0 0.1 squeeze.88
  18.1 0.1 squeeze.87
  18.2 0.1 squeeze.86
  18.4 0.1 squeeze.85
  18.5 0.1 squeeze.84
  18.6 0.1 squeeze.83
  18.8 0.1 squeeze.82
  18.9 0.2 add_convert_fusion
  19.1 0.6 copy.46
  19.8 0.6 constant_dynamic-slice_fusion.16
  23.1 0.8 fusion.16
  33.8 0.7 reshape.284
  39.6 0.2 convolution_bitcast_fusion
  39.9 0.7 pad_multiply_fusion
  40.6 0.7 pad_multiply_fusion.1
  41.4 0.7 multiply_divide_fusion
  42.1 59.6 %all-gather.6.cloned.1.call-done = bf16[128,1,3,4096]{3,2,1,0:T(4,128)(2,1)} async-done(((bf16[1,1,3,4096]{3,2,1,0:T(4,128)(2,1)}), bf16[128,1,3,4096]{3,2,1,0:T(4,128)(2,1)}) %all-gather.6.cloned.1.call-update) | async-done | bytes 3145744 | tf_op jit(solution)/shard_map/all_gather | solution.py:90
  101.8 1.0 constant_dynamic-slice_fusion.7
  102.7 0.1 reshape.280
  102.8 0.6 slice.214
  103.6 0.6 slice.213
  104.3 0.7 slice.212
  104.9 0.7 reshape.277
  105.8 0.7 slice.210
  106.6 0.6 slice.209
  107.2 0.1 reshape.274
  107.3 0.6 slice.208
  107.9 0.7 reshape.273
  108.6 1.0 slice.207
  109.6 1.3 convert_reduce_fusion
  110.8 0.7 bitcast_dynamic-update-slice_fusion.8
  111.6 0.6 bitcast_dynamic-update-slice_fusion.7
  112.2 0.7 bitcast_dynamic-update-slice_fusion.6
  112.9 0.7 bitcast_dynamic-update-slice_fusion.5
  113.6 0.6 bitcast_dynamic-update-slice_fusion.4
  114.2 0.7 bitcast_dynamic-update-slice_fusion.3
  114.9 0.7 bitcast_dynamic-update-slice_fusion.2
  115.7 0.6 bitcast_dynamic-update-slice_fusion.1
  116.3 0.7 bitcast_dynamic-update-slice_fusion
  117.0 2.1 reshape.307
  119.1 3.2 %fusion = bf16[1,1,96,3,4096]{4,2,3,1,0:T(8,128)(2,1)} fusion(bf16[27,4096,1]{1,0,2:T(8,128)(2,1)} %reshape.307, bf16[3,27,96]{2,1,0:T(8,128)(2,1)} %copy-done.3), kind=kOutput, calls=%fused_computation.1 | convolution fusion | flops 64880640 | bytes 2596032 | tf_op jit(solution)/shard_map/tjc,jp->ctp/dot_general | solution.py:122
  122.3 1.5 fusion.8
  123.8 62.6 %all-gather.4.cloned.1.call-done = bf16[128,3,4096]{2,1,0:T(4,128)(2,1)} async-done(((bf16[1,3,4096]{2,1,0:T(4,128)(2,1)}), bf16[128,3,4096]{2,1,0:T(4,128)(2,1)}) %all-gather.4.cloned.1.call-update) | async-done | bytes 3145744 | tf_op jit(solution)/shard_map/all_gather | solution.py:87
  186.4 1.0 constant_dynamic-slice_fusion.15
  187.4 0.1 reshape.271
  187.5 0.1 reshape.270
  187.6 0.1 reshape.269
  187.9 0.1 reshape.268
  188.0 0.1 reshape.267
  188.3 0.1 reshape.266
  188.4 0.1 reshape.265
  188.5 0.1 reshape.264
  188.7 1.5 fusion.12
  190.3 0.7 reshape.272
  191.0 96.1 %all-reduce.26 = (f32[3,27,96]{2,1,0:T(8,128)S(1)}, f32[3]{0:T(128)S(1)}) all-reduce(f32[3,27,96]{2,1,0:T(8,128)S(1)} %copy-done.4, f32[3]{0:T(128)S(1)} %get-tuple-element.14), channel_id=1, replica_groups=mesh['tile'=128,'clip'=4] {'tile','clip'}, use_global_device_ids=true, to_apply=%region_8.9 | all-reduce | flops 7779 | bytes 62232 | tf_op jit(solution)/shard_map/psum | solution.py:126
  287.1 0.6 reshape.283
  287.8 0.5 broadcast_multiply_fusion.2
  (59 shorter events, 1.4 us)
Async XLA Ops:
  7.2 94.6 %all-gather.6.cloned.1.call-start = ((), (), s32[]{:S(2)}) async-start(), calls=%async_computation.1 | async-start | bytes 4227072 | tf_op jit(solution)/shard_map/all_gather | solution.py:90
  7.9 4.6 %copy-start.6 = (bf16[3,9,3,96]{3,2,1,0:T(4,128)(2,1)S(1)}, bf16[3,9,3,96]{3,2,1,0:T(4,128)(2,1)}, u32[]{:S(2)}) copy-start(bf16[3,9,3,96]{3,2,1,0:T(4,128)(2,1)} %param.7) | copy-start | bytes 46660
  7.9 178.5 %all-gather.4.cloned.1.call-start = ((), (), s32[]{:S(2)}) async-start(), calls=%async_computation | async-start | bytes 4227072 | tf_op jit(solution)/shard_map/all_gather | solution.py:87
  12.5 0.6 copy-start.3
  17.1 1.7 copy-start.7
  17.6 2.2 copy-start.8
  17.7 16.2 %copy-start.5 = (bf16[1,1,3,4096]{3,2,1,0:T(4,128)(2,1)S(1)}, bf16[1,1,3,4096]{3,2,1,0:T(4,128)(2,1)}, u32[]{:S(2)}) copy-start(bf16[1,1,3,4096]{3,2,1,0:T(4,128)(2,1)} %param.11) | copy-start | bytes 73732
  17.7 21.9 %copy-start.9 = (s32[32]{0:T(128)S(1)}, s32[32]{0:T(128)}, u32[]{:S(2)}) copy-start(s32[32]{0:T(128)} %param.9) | copy-start | bytes 388
  39.9 1.4 copy-start.2
  108.6 13.7 %copy-start = (bf16[1,1,96,3,4096]{4,2,3,1,0:T(8,128)(2,1)S(1)}, bf16[1,1,96,3,4096]{4,2,3,1,0:T(8,128)(2,1)}, u32[]{:S(2)}) copy-start(bf16[1,1,96,3,4096]{4,2,3,1,0:T(8,128)(2,1)} %param.6) | copy-start | bytes 7077892
  119.1 3.3 %copy-start.1 = (bf16[27,4096,1]{1,0,2:T(8,128)(2,1)S(1)}, bf16[27,4096,1]{1,0,2:T(8,128)(2,1)}, u32[]{:S(2)}) copy-start(bf16[27,4096,1]{1,0,2:T(8,128)(2,1)} %reshape.307) | copy-start | bytes 663556
  123.8 67.2 %copy-start.4 = (f32[3,27,96]{2,1,0:T(8,128)S(1)}, f32[3,27,96]{2,1,0:T(8,128)}, u32[]{:S(2)}) copy-start(f32[3,27,96]{2,1,0:T(8,128)} %fusion.8) | copy-start | bytes 93316
Sparse Core Ops, SparseCore 0:
  11.1 90.5 all-gather.5
  104.9 81.4 all-gather.3
where the time goes:
time: 296 us; the launch traced here: 295 us
  waiting for transfers between devices  123 us (42%)
  blocking collectives  96.1 us (32%)
  between operations  32 us (11%)
  local copies, waits for them, and re-layouts  28.5 us (10%)
  matrix products  8.93 us (3%)
  other arithmetic  6.52 us (2%)
    psum x1, blocking collectives, per_device(): lax.psum((kernel_local, bias_local), ('tile', 'clip'))  96.1 us
    all_gather x1, waiting for transfers between devices, per_device(): lax.all_gather(tile_image.reshape(1, colours, pixels), 'tile', axis=0, ti...  62.6 us
    all_gather x1, waiting for transfers between devices, per_device(): lax.all_gather(cotangent.reshape(1, colours, pixels), 'tile', axis=0, til...  59.6 us
    unnamed x37, local copies, waits for them, and re-layouts  10.8 us
  transfers between devices with their start and end apart: 2, of which 2 were waited for; matrix products, arithmetic and copies ran while one was open for 13% of the time, Pallas kernels for 0%

commit v1 on v0

--- a/solution.py
+++ b/solution.py
@@ -87,8 +87,11 @@
     gathered_images = lax.all_gather(
         tile_image.reshape(1, colours, pixels), "tile", axis=0, tiled=True
     )
-    gathered_grads = lax.all_gather(
-        cotangent.reshape(1, colours, pixels), "tile", axis=0, tiled=True
+    gathered_grads = jnp.concatenate(
+        lax.all_to_all(
+            jnp.stack([cotangent.reshape(1, colours, pixels)] * lax.axis_size("tile")), "tile", 0, 0
+        ),
+        axis=0,
     )
     forward_regions = pick_regions(gathered_images, neighbours, intersection, edge)
     backward_regions = pick_regions(gathered_grads, neighbours, intersection, edge)

time: 296 us -> 284 us (0.959)
  waiting for transfers between devices: 123 us -> 34.5 us
  local copies, waits for them, and re-layouts: 28.5 us -> 75.4 us
  starting transfers between devices: 0.08 us -> 19.1 us
  blocking collectives: 96.1 us -> 105 us
    all_gather x1, waiting for transfers between devices: 62.6 us -> 0.01 us  [per_device(): lax.all_gather(tile_image.reshape(1, colours, pixels), 'tile', axis=0, ti...]
    all_gather x1 -> x0, waiting for transfers between devices: 59.6 us -> none  [per_device(): lax.all_gather(cotangent.reshape(1, colours, pixels), 'tile', axis=0, til...]
    all_to_all x0 -> x1, waiting for transfers between devices: none -> 34.4 us  [per_device(): lax.all_to_all(jnp.stack([cotangent.reshape(1, colours, pixels)] * lax.ax...]
    all_to_all x0 -> x1, starting transfers between devices: none -> 19 us  [per_device(): lax.all_to_all(jnp.stack([cotangent.reshape(1, colours, pixels)] * lax.ax...]
    slice x10, local copies, waits for them, and re-layouts: 0.55 us -> 14.4 us  [per_device(): padded[shift_y, shift_x, :, shift_y:shift_y + edge, shift_x:shift_x + edge]]
    squeeze x9, local copies, waits for them, and re-layouts: 1 us -> 14.6 us  [per_device(): padded[shift_y, shift_x, :, shift_y:shift_y + edge, shift_x:shift_x + edge]]
    reshape x16, local copies, waits for them, and re-layouts: 2.87 us -> 12.7 us  [pick_regions(): whole_tile = whole_tile.reshape(whole_tile.shape[0], edge, edge)]
    psum x1, blocking collectives: 96.1 us -> 105 us  [per_device(): lax.psum((kernel_local, bias_local), ('tile', 'clip'))]
  transfers between devices with their start and end apart: 2 -> 2, of which waited for: 2 -> 1; matrix products, arithmetic and copies ran while one was open for 13% -> 30% of each run, Pallas kernels for 0% -> 0%
where the time goes in v1:
time: 284 us; the launch traced here: 282 us
  blocking collectives  105 us (37%)
  local copies, waits for them, and re-layouts  75.4 us (27%)
  waiting for transfers between devices  34.5 us (12%)
  between operations  32 us (11%)
  starting transfers between devices  19.1 us (7%)
  matrix products  9.89 us (3%)
  other arithmetic  6.58 us (2%)
    psum x1, blocking collectives, per_device(): lax.psum((kernel_local, bias_local), ('tile', 'clip'))  105 us
    all_to_all x1, waiting for transfers between devices, per_device(): lax.all_to_all(jnp.stack([cotangent.reshape(1, colours, pixels)] * lax.ax...  34.4 us
    all_to_all x1, starting transfers between devices, per_device(): lax.all_to_all(jnp.stack([cotangent.reshape(1, colours, pixels)] * lax.ax...  19 us
    squeeze x9, local copies, waits for them, and re-layouts, per_device(): padded[shift_y, shift_x, :, shift_y:shift_y + edge, shift_x:shift_x + edge]  14.6 us
    slice x10, local copies, waits for them, and re-layouts, per_device(): padded[shift_y, shift_x, :, shift_y:shift_y + edge, shift_x:shift_x + edge]  14.4 us
    reshape x16, local copies, waits for them, and re-layouts, pick_regions(): whole_tile = whole_tile.reshape(whole_tile.shape[0], edge, edge)  12.7 us
    unnamed x51, local copies, waits for them, and re-layouts  8.51 us
  transfers between devices with their start and end apart: 2, of which 1 were waited for; matrix products, arithmetic and copies ran while one was open for 30% of the time, Pallas kernels for 0%

profile of v1, /device:TPU:1, one launch (start us, length us, event | category | flops | bytes accessed | tf_op | source)
XLA Modules:
  0.0 282.0 jit_solution(2601668774430020179)
XLA Ops:
  7.2 4.8 %stack.33 = bf16[128,1,3,4096]{3,2,1,0:T(4,128)(2,1)} broadcast(bf16[3,4096]{1,0:T(4,128)(2,1)} %bitcast.187), dimensions={2,3} | broadcast | bytes 3170304 | tf_op jit(solution)/shard_map/stack | solution.py:92
  12.0 19.0 %all-to-all-start = ((bf16[128,1,3,4096]{3,2,1,0:T(4,128)(2,1)}), bf16[128,1,3,4096]{3,2,1,0:T(4,128)(2,1)}, u32[]{:S(2)}, u32[]{:S(2)}) async-start(bf16[128,1,3,4096]{3,2,1,0:T(4,128)(2,1)} %stack.33), calls=%async_computation | async-start | bytes 8388608 | tf_op jit(solution)/shard_map/all_to_all | solution.py:91
  31.1 0.6 dot_general.22
  31.7 2.8 copy.34
  34.5 4.0 %fusion.5 = f32[3,3,3,64,64]{4,2,3,1,0:T(4,128)S(1)} fusion(bf16[64,64,96,3,1,1]{2,1,0,3,5,4:T(8,128)(2,1)} %bitcast.183, bf16[3,3,3,96,3]{3,2,1,0,4:T(4,128)(2,1)} %dot_general.22), kind=kOutput, calls=%fused_computation.6 | convolution fusion | flops 63700992 | bytes 2817216 | tf_op jit(solution)/shard_map/tjc,ctp->jp/dot_general | solution.py:75
  38.6 1.4 pad_slice_fusion.7
  40.0 0.6 copy.37
  40.6 1.6 squeeze.82
  42.2 1.5 copy.38
  43.8 1.6 squeeze.83
  45.4 1.6 copy.39
  46.9 1.6 squeeze.84
  48.6 1.6 copy.40
  50.1 1.6 squeeze.85
  51.7 1.6 copy.41
  53.3 1.6 squeeze.86
  54.9 1.6 copy.42
  56.5 1.6 squeeze.87
  58.1 1.6 copy.43
  59.6 1.6 squeeze.88
  61.3 1.6 copy.44
  62.8 1.6 squeeze.89
  64.4 1.6 copy.45
  66.0 1.6 squeeze.90
  67.6 1.2 add_convert_fusion
  68.8 0.7 copy.46
  72.7 0.8 fusion.16
  83.5 1.5 reshape.304
  90.4 0.7 pad_multiply_fusion.1
  91.1 0.7 pad_multiply_fusion
  91.9 0.7 multiply_divide_fusion
  92.6 34.4 %all-to-all-done = bf16[128,1,3,4096]{3,2,1,0:T(4,128)(2,1)} async-done(((bf16[128,1,3,4096]{3,2,1,0:T(4,128)(2,1)}), bf16[128,1,3,4096]{3,2,1,0:T(4,128)(2,1)}, u32[]{:S(2)}, u32[]{:S(2)}) %all-to-all-start) | async-done | bytes 3145760 | tf_op jit(solution)/shard_map/all_to_all | solution.py:91
  127.1 1.6 constant_dynamic-slice_fusion.7
  128.7 1.5 reshape.296
  130.2 1.5 slice.210
  131.7 1.5 reshape.293
  133.1 1.4 slice.207
  134.6 1.5 reshape.294
  136.0 1.3 slice.208
  137.4 1.5 reshape.295
  138.9 1.3 slice.209
  140.2 1.5 reshape.298
  141.7 1.4 slice.212
  143.1 1.5 reshape.299
  144.6 1.3 slice.213
  146.0 1.5 reshape.300
  147.4 1.3 slice.214
  148.8 1.5 reshape.297
  150.3 1.3 convert_reduce_fusion
  151.5 0.7 bitcast_dynamic-update-slice_fusion.8
  152.2 0.6 bitcast_dynamic-update-slice_fusion.7
  152.9 0.7 bitcast_dynamic-update-slice_fusion.6
  153.6 0.7 bitcast_dynamic-update-slice_fusion.5
  154.9 0.7 bitcast_dynamic-update-slice_fusion.3
  155.6 0.7 bitcast_dynamic-update-slice_fusion.2
  156.3 0.6 bitcast_dynamic-update-slice_fusion.1
  157.0 0.7 bitcast_dynamic-update-slice_fusion
  157.7 2.1 reshape.310
  159.8 2.4 fusion.8
  162.2 104.7 %all-reduce.26 = (f32[3,27,96]{2,1,0:T(8,128)S(1)}, f32[3]{0:T(128)S(1)}) all-reduce(f32[3,27,96]{2,1,0:T(8,128)} %fusion.8, f32[3]{0:T(128)S(1)} %get-tuple-element.14), channel_id=1, replica_groups=mesh['tile'=128,'clip'=4] {'tile','clip'}, use_global_device_ids=true, to_apply=%region_8.9 | all-reduce | flops 7779 | bytes 62232 | tf_op jit(solution)/shard_map/psum | solution.py:129
  266.9 0.6 reshape.303
  267.6 3.3 %fusion = bf16[1,1,96,3,4096]{4,2,3,1,0:T(8,128)(2,1)} fusion(bf16[27,4096,1]{1,0,2:T(8,128)(2,1)} %reshape.310, bf16[3,27,96]{2,1,0:T(8,128)(2,1)} %copy-done.3), kind=kOutput, calls=%fused_computation.1 | convolution fusion | flops 64880640 | bytes 2596032 | tf_op jit(solution)/shard_map/tjc,jp->ctp/dot_general | solution.py:125
  271.4 1.0 constant_dynamic-slice_fusion.15
  274.5 0.7 reshape.292
  (73 shorter events, 4.2 us)
Async XLA Ops:
  12.0 19.1 %copy-start.13 = (bf16[3,9,3,96]{3,2,1,0:T(4,128)(2,1)S(1)}, bf16[3,9,3,96]{3,2,1,0:T(4,128)(2,1)}, u32[]{:S(2)}) copy-start(bf16[3,9,3,96]{3,2,1,0:T(4,128)(2,1)} %param.7) | copy-start | bytes 46660
  12.0 19.8 %copy-start = (bf16[1,1,96,3,4096]{4,2,3,1,0:T(8,128)(2,1)S(1)}, bf16[1,1,96,3,4096]{4,2,3,1,0:T(8,128)(2,1)}, u32[]{:S(2)}) copy-start(bf16[1,1,96,3,4096]{4,2,3,1,0:T(8,128)(2,1)} %param.6) | copy-start | bytes 7077892
  12.0 115.1 %all-to-all-start = ((bf16[128,1,3,4096]{3,2,1,0:T(4,128)(2,1)}), bf16[128,1,3,4096]{3,2,1,0:T(4,128)(2,1)}, u32[]{:S(2)}, u32[]{:S(2)}) async-start(bf16[128,1,3,4096]{3,2,1,0:T(4,128)(2,1)} %stack.33), calls=%async_computation | async-start | bytes 8388608 | tf_op jit(solution)/shard_map/all_to_all | solution.py:91
  31.0 240.4 %all-gather.2.cloned.1.call-start = ((), (), s32[]{:S(2)}) async-start(), calls=%async_computation.1 | async-start | bytes 4227072 | tf_op jit(solution)/shard_map/all_gather | solution.py:87
  31.1 3.4 %copy-start.3 = (bf16[3,27,96]{2,1,0:T(8,128)(2,1)}, bf16[3,27,96]{2,1,0:T(8,128)(2,1)S(1)}, u32[]{:S(2)}) copy-start(bf16[3,27,96]{2,1,0:T(8,128)(2,1)S(1)} %reshape.283) | copy-start | bytes 46660
  38.6 29.0 %copy-start.14 = (f32[3]{0:T(128)S(1)}, f32[3]{0:T(128)}, u32[]{:S(2)}) copy-start(f32[3]{0:T(128)} %param.8) | copy-start | bytes 40
  40.0 29.6 %copy-start.15 = (s32[1,128]{1,0:T(1,128)S(1)}, s32[1,128]{1,0:T(1,128)}, u32[]{:S(2)}) copy-start(s32[1,128]{1,0:T(1,128)} %param.10) | copy-start | bytes 1540
  40.0 50.1 %copy-start.16 = (s32[32]{0:T(128)S(1)}, s32[32]{0:T(128)}, u32[]{:S(2)}) copy-start(s32[32]{0:T(128)} %param.9) | copy-start | bytes 388
  90.3 1.5 copy-start.1
  267.5 6.2 %copy-start.2 = (f32[64,64]{1,0:T(8,128)S(1)}, f32[64,64]{1,0:T(8,128)}, u32[]{:S(2)}) copy-start(f32[64,64]{1,0:T(8,128)} %copy-done.1) | copy-start | bytes 49156
  267.5 6.2 %copy-start.4 = (f32[64,64]{1,0:T(8,128)S(1)}, f32[64,64]{1,0:T(8,128)}, u32[]{:S(2)}) copy-start(f32[64,64]{1,0:T(8,128)} %get-tuple-element.57) | copy-start | bytes 49156
  267.5 6.2 %copy-start.5 = (f32[64,64]{1,0:T(8,128)S(1)}, f32[64,64]{1,0:T(8,128)}, u32[]{:S(2)}) copy-start(f32[64,64]{1,0:T(8,128)} %get-tuple-element.58) | copy-start | bytes 49156
  267.5 6.2 %copy-start.6 = (f32[64,64]{1,0:T(8,128)S(1)}, f32[64,64]{1,0:T(8,128)}, u32[]{:S(2)}) copy-start(f32[64,64]{1,0:T(8,128)} %get-tuple-element.55) | copy-start | bytes 49156
  267.5 6.2 %copy-start.7 = (f32[64,64]{1,0:T(8,128)S(1)}, f32[64,64]{1,0:T(8,128)}, u32[]{:S(2)}) copy-start(f32[64,64]{1,0:T(8,128)} %get-tuple-element.56) | copy-start | bytes 49156
  267.5 6.2 %copy-start.8 = (f32[64,64]{1,0:T(8,128)S(1)}, f32[64,64]{1,0:T(8,128)}, u32[]{:S(2)}) copy-start(f32[64,64]{1,0:T(8,128)} %get-tuple-element.17) | copy-start | bytes 49156
  267.5 6.2 %copy-start.9 = (f32[64,64]{1,0:T(8,128)S(1)}, f32[64,64]{1,0:T(8,128)}, u32[]{:S(2)}) copy-start(f32[64,64]{1,0:T(8,128)} %get-tuple-element.18) | copy-start | bytes 49156
  267.6 6.2 %copy-start.10 = (f32[64,64]{1,0:T(8,128)S(1)}, f32[64,64]{1,0:T(8,128)}, u32[]{:S(2)}) copy-start(f32[64,64]{1,0:T(8,128)} %get-tuple-element.19) | copy-start | bytes 49156
  267.6 6.2 %copy-start.11 = (f32[64,64]{1,0:T(8,128)S(1)}, f32[64,64]{1,0:T(8,128)}, u32[]{:S(2)}) copy-start(f32[64,64]{1,0:T(8,128)} %get-tuple-element.53) | copy-start | bytes 49156
  267.6 6.2 %copy-start.12 = (f32[64,64]{1,0:T(8,128)S(1)}, f32[64,64]{1,0:T(8,128)}, u32[]{:S(2)}) copy-start(f32[64,64]{1,0:T(8,128)} %get-tuple-element.54) | copy-start | bytes 49156
Sparse Core Ops, SparseCore 0:
  69.6 119.1 all-gather.1
